TPU v7x, 256 devices: a whole 4x4x8 slice. The times are simulated.
256 devices in a mesh: row: 32 (over x, y, core), col: 8 (over z).
Axes of the slice: x: 4, y: 4, z: 8, core: 2. Of those that a mesh axis runs over, the one named last changes fastest.
Arguments:
- in_map: bfloat16 [512, 256, 256], P('row', 'col'), may hold values from -6 to 6
- tile_w: bfloat16 [3, 3, 256, 256], replicated, may hold values from -0.125 to 0.125
- head_w1: bfloat16 [3, 3, 256, 256], replicated, may hold values from -0.125 to 0.125
- head_w2: bfloat16 [3, 3, 256, 256], replicated, may hold values from -0.125 to 0.125
- box_row: int32 [512, 8], P('row', 'col'), may hold values from 0 to 2
- box_col: int32 [512, 8], P('row', 'col'), may hold values from 0 to 18
- box_target: int32 [512, 8], P('row', 'col'), may hold values from -1 to 31, as said below
- head_cot: bfloat16 [128, 8, 14, 14, 256], P('row', 'col'), may hold values from -6 to 6
Outputs:
- grad_map: bfloat16 [512, 256, 256], P('row', 'col')
- grad_w1: float32 [3, 3, 256, 256], replicated
- grad_w2: float32 [3, 3, 256, 256], replicated
Inputs may be any that keep to these rules, and one draw needn't show every extreme that they name: `box_target`: within each row r of tiles, every head slot d * 4 + h (d below 8, h below 4) is named by exactly one tile slot, and empty slots hold -1. A tile names at most 2 head slots of one device, so it holds at most 16 boxes; in every row of tiles one tile holds 16 boxes, 2 for each device of the row.
All inputs are finite; a program needn't handle non-finite values.
Results may differ from a plain program's by a relative error of at most 0.012.
Values may be sent and summed in bfloat16 or wider, within the bound.
A program may use at most 64 MiB of HBM per device.

v0:
```python
import math
import jax
import jax.numpy as jnp
from jax import lax
from jax.sharding import PartitionSpec as P

LAYOUT = ("NHWC", "HWIO", "NHWC")


def padded_2(shard, sides, width):
    for axis, dim in sides:
        size, length = (lax.axis_size(axis), shard.shape[dim])
        up = [(i, (i + 1) % size) for i in range(size - 1)]
        down = [(j, i) for i, j in up]
        last = lax.slice_in_dim(shard, length - width, length, axis=dim)
        leading = lax.slice_in_dim(shard, 0, width, axis=dim)
        before = lax.ppermute(last, axis, up)
        after = lax.ppermute(leading, axis, down)
        shard = jnp.concatenate([before, shard, after], axis=dim)
    return shard


def conv_pad(inputs, kernel, margin):
    return lax.conv_general_dilated(
        inputs,
        kernel,
        (1, 1),
        ((margin, margin), (margin, margin)),
        dimension_numbers=LAYOUT,
        preferred_element_type=jnp.float32,
    )


def flip_weights(kernel):
    return jnp.transpose(jnp.flip(kernel, (0, 1)), (0, 1, 3, 2))


def silu_slope(values):
    sigma = jax.nn.sigmoid(values)
    return sigma * (1.0 + values * (1.0 - sigma))


def weight_grad(inputs, deltas):
    channels = inputs.shape[-1]
    box_side = inputs.shape[1]
    padded = jnp.pad(inputs, ((0, 0), (1, 1), (1, 1), (0, 0)))
    flat_delta = deltas.reshape(-1, channels)
    blocks = []
    for shift_y in range(3):
        for shift_x in range(3):
            window = padded[
                :, shift_y : shift_y + box_side, shift_x : shift_x + box_side, :
            ].reshape(-1, channels)
            blocks.append(
                lax.dot_general(
                    window, flat_delta, (((0,), (0,)), ((), ())), preferred_element_type=jnp.float32
                )
            )
    return jnp.stack(blocks).reshape(3, 3, channels, channels)


def pick_rows(table, values):
    flat = values.reshape(values.shape[0], -1)
    return jnp.dot(table, flat, preferred_element_type=jnp.float32).astype(jnp.bfloat16)


def pick_back(table, values):
    return lax.dot_general(
        table, values, (((0,), (0,)), ((), ())), preferred_element_type=jnp.float32
    ).astype(jnp.bfloat16)


def body(in_map, tile_w, head_w1, head_w2, box_row, box_col, box_target, head_cot):
    tile_rows, tile_cols, channels = in_map.shape
    head_count = head_cot.shape[0]
    box_side = head_cot.shape[2]
    slot_count = box_target.shape[0]
    columns = lax.axis_size("col")
    capacity = slot_count // columns
    pair_count = columns * capacity
    padded = padded_2(in_map, (("row", 0), ("col", 1)), 1)
    preact = conv_pad(padded[None], tile_w, 0)[0]
    target = box_target[:, 0]
    occupied = target >= 0
    dest_col = jnp.where(occupied, target // head_count, 0)
    head_slot = jnp.where(occupied, target % head_count, 0)
    slot_ids = jnp.arange(slot_count, dtype=jnp.int32)
    same_dest = (dest_col[:, None] == dest_col[None, :]) & occupied[None, :]
    placing = jnp.sum(same_dest & (slot_ids[None, :] < slot_ids[:, None]), axis=1)
    pair_slot = dest_col * capacity + placing
    pair_ids = jnp.arange(pair_count, dtype=jnp.int32)
    send_map = ((pair_slot[None, :] == pair_ids[:, None]) & occupied[None, :]).astype(jnp.bfloat16)
    head_ids = jnp.arange(head_count, dtype=jnp.int32)
    head_hot = ((head_slot[:, None] == head_ids[None, :]) & occupied[:, None]).astype(jnp.bfloat16)
    pair_head = (
        jnp.dot(send_map, head_hot, preferred_element_type=jnp.float32)
        .astype(jnp.bfloat16)
        .reshape(columns, capacity, head_count)
    )
    top_row = box_row[:, 0]
    left_col = box_col[:, 0]
    zero_index = jnp.zeros((), jnp.int32)
    feature = jax.nn.silu(preact).astype(jnp.bfloat16)
    crops = jax.vmap(
        lambda y, x: lax.dynamic_slice(feature, (y, x, zero_index), (box_side, box_side, channels))
    )(top_row, left_col)
    outgoing = pick_rows(send_map, crops).reshape(columns, capacity, box_side, box_side, channels)
    arrived, arrived_head = (
        lax.all_to_all(outgoing, "col", split_axis=0, concat_axis=0, tiled=True),
        lax.all_to_all(pair_head, "col", split_axis=0, concat_axis=0, tiled=True),
    )
    arrived_head = arrived_head.reshape(pair_count, head_count)
    box_input = pick_back(arrived_head, arrived.reshape(pair_count, -1)).reshape(
        head_count, box_side, box_side, channels
    )
    factor = 1.0 / math.sqrt(lax.axis_size("row") * columns * head_count * box_side * box_side)
    cotangent = head_cot[:, 0]
    pre_one = conv_pad(box_input, head_w1, 1)
    hidden = jax.nn.silu(pre_one).astype(jnp.bfloat16)
    pre_two = conv_pad(hidden, head_w2, 1)
    delta_two = (cotangent.astype(jnp.float32) * silu_slope(pre_two)).astype(jnp.bfloat16)
    second_local = weight_grad(hidden, delta_two)
    delta_one = (conv_pad(delta_two, flip_weights(head_w2), 1) * silu_slope(pre_one)).astype(
        jnp.bfloat16
    )
    box_grads = conv_pad(delta_one, flip_weights(head_w1), 1).astype(jnp.bfloat16)
    sent_back = pick_rows(arrived_head, box_grads).reshape(
        columns, capacity, box_side, box_side, channels
    )
    returned = lax.all_to_all(sent_back, "col", split_axis=0, concat_axis=0, tiled=True)
    slot_grads = pick_back(send_map, returned.reshape(pair_count, -1)).reshape(
        slot_count, box_side, box_side, channels
    )
    first_local = weight_grad(box_input, delta_one)
    first_sum, second_sum = lax.psum((first_local, second_local), ("row", "col"))

    def add_box(slot, running):
        current = lax.dynamic_slice(
            running, (top_row[slot], left_col[slot], zero_index), (box_side, box_side, channels)
        )
        return lax.dynamic_update_slice(
            running,
            current + slot_grads[slot].astype(jnp.float32),
            (top_row[slot], left_col[slot], zero_index),
        )

    box_total = lax.fori_loop(
        0, slot_count, add_box, jnp.zeros((tile_rows, tile_cols, channels), jnp.float32)
    )
    delta_map = (box_total * silu_slope(preact)).astype(jnp.bfloat16)
    delta_rim = padded_2(delta_map, (("row", 0), ("col", 1)), 1)
    grad_map = conv_pad(delta_rim[None], flip_weights(tile_w), 0)[0].astype(jnp.bfloat16)
    return (grad_map, first_sum * factor, second_sum * factor)


def solution(mesh):
    in_specs = (
        P("row", "col", None),
        P(),
        P(),
        P(),
        P("row", "col"),
        P("row", "col"),
        P("row", "col"),
        P("row", "col", None, None, None),
    )
    out_specs = (P("row", "col", None), P(), P())
    return jax.shard_map(body, mesh=mesh, in_specs=in_specs, out_specs=out_specs, check_vma=False)
```

profile of v0, /device:TPU:98, one launch (start us, length us, event | category | flops | bytes accessed | tf_op | source)
XLA Modules:
  0.0 488.1 jit_solution(9538092367469643481)
XLA Ops:
  8.0 4.3 collective-permute-start.1
  12.3 1.9 collective-permute-start
  17.8 1.7 collective-permute-done
  20.6 5.2 %collective-permute-start.2 = (bf16[18,1,256]{2,1,0:T(2,128)(2,1)S(1)}, bf16[18,1,256]{2,1,0:T(2,128)(2,1)S(1)}, u32[]{:S(2)}, u32[]{:S(2)}) collective-permute-start(bf16[18,1,256]{2,1,0:T(2,128)(2,1)S(1)} %get-tuple-element.157), channel_id=1, source_target_pairs={{0,1},{1,2},{2,3},{3,4},{4,5},{5,6},{6,7},{8,9},{9,10},{10,11},{11... | collective-permute-start | bytes 27656 | tf_op jit(solution)/shard_map/ppermute | solution.py:17
  25.7 1.9 collective-permute-start.3
  27.7 4.9 %collective-permute-done.3 = bf16[18,1,256]{2,1,0:T(2,128)(2,1)S(1)} collective-permute-done((bf16[18,1,256]{2,1,0:T(2,128)(2,1)S(1)}, bf16[18,1,256]{2,1,0:T(2,128)(2,1)S(1)}, u32[]{:S(2)}, u32[]{:S(2)}) %collective-permute-start.3) | collective-permute-done | bytes 9248 | tf_op jit(solution)/shard_map/ppermute | solution.py:18
  35.2 41.9 %while.15 = (s32[]{:T(128)}, bf16[16,32,256]{2,0,1:T(8,128)(2,1)S(1)}, s32[16,3]{0,1:T(4,128)S(1)}, bf16[16,14,14,256]{3,2,1,0:T(8,128)(2,1)}, s32[]{:T(128)}) while((s32[]{:T(128)}, bf16[16,32,256]{2,0,1:T(8,128)(2,1)S(1)}, s32[16,3]{0,1:T(4,128)S(1)}, bf16[16,14,14,256]{3,2,1,0:T(8,128)(2,1)}, s32[]{:T(128)}) %tuple.61), condition=%wide.while_cond, body=%wide.while_body.sunk | while | flops 2 | bytes 415869 | solution.py:105
  35.9 1.3 constant_dynamic-slice_fusion.8
  38.5 1.3 constant_dynamic-slice_fusion.8
  41.1 1.3 constant_dynamic-slice_fusion.8
  43.7 1.3 constant_dynamic-slice_fusion.8
  46.3 1.3 constant_dynamic-slice_fusion.8
  49.0 1.3 constant_dynamic-slice_fusion.8
  51.6 1.3 constant_dynamic-slice_fusion.8
  54.2 1.3 constant_dynamic-slice_fusion.8
  56.8 1.3 constant_dynamic-slice_fusion.8
  59.4 1.3 constant_dynamic-slice_fusion.8
  62.1 1.3 constant_dynamic-slice_fusion.8
  64.7 1.3 constant_dynamic-slice_fusion.8
  67.3 1.3 constant_dynamic-slice_fusion.8
  69.9 1.3 constant_dynamic-slice_fusion.8
  72.5 1.3 constant_dynamic-slice_fusion.8
  75.2 1.3 constant_dynamic-slice_fusion.8
  77.2 2.4 reshape.125
  79.6 1.7 convolution_convert_fusion.1
  81.3 2.6 reshape.126
  83.9 3.6 copy.100
  87.6 5.2 %all-to-all-start.1 = ((bf16[8,2,14,14,256]{4,1,3,2,0:T(2,128)(2,1)}), bf16[8,2,14,14,256]{4,1,3,2,0:T(2,128)(2,1)}, u32[]{:S(2)}, u32[]{:S(2)}) async-start(bf16[8,2,14,14,256]{4,1,3,2,0:T(2,128)(2,1)} %copy.100), calls=%async_computation.1 | async-start | bytes 3211264 | tf_op jit(solution)/shard_map/all_to_all | solution.py:109
  93.8 32.7 %all-to-all-done.1 = bf16[8,2,14,14,256]{4,1,3,2,0:T(2,128)(2,1)} async-done(((bf16[8,2,14,14,256]{4,1,3,2,0:T(2,128)(2,1)}), bf16[8,2,14,14,256]{4,1,3,2,0:T(2,128)(2,1)}, u32[]{:S(2)}, u32[]{:S(2)}) %all-to-all-start.1) | async-done | bytes 1605664 | tf_op jit(solution)/shard_map/all_to_all | solution.py:109
  126.4 6.7 %all-to-all-start = ((bf16[8,2,4]{2,1,0:T(2,128)(2,1)}), bf16[8,2,4]{2,1,0:T(2,128)(2,1)S(1)}, u32[]{:S(2)}, u32[]{:S(2)}) async-start(bf16[8,2,4]{2,1,0:T(2,128)(2,1)} %bitcast.9), calls=%async_computation | async-start | bytes 8192 | tf_op jit(solution)/shard_map/all_to_all | solution.py:110
  133.1 1.7 copy.101
  134.8 2.1 reshape.127
  137.5 1.8 convolution_convert_fusion.3
  142.2 1.2 convolution_select_fusion.1
  143.5 1.1 select_bitcast_fusion.1
  144.7 1.3 add_multiply_fusion
  147.3 1.2 fusion.51
  150.5 1.3 fusion.8
  152.7 1.1 fusion.27
  156.2 1.3 convolution_convert_fusion.4
  159.0 1.7 reshape.130
  160.7 3.7 copy.109
  164.4 6.9 %all-to-all-start.2 = ((bf16[8,2,14,14,256]{4,1,3,2,0:T(2,128)(2,1)}), bf16[8,2,14,14,256]{4,1,3,2,0:T(2,128)(2,1)S(1)}, u32[]{:S(2)}, u32[]{:S(2)}) async-start(bf16[8,2,14,14,256]{4,1,3,2,0:T(2,128)(2,1)} %copy.109), calls=%async_computation.2 | async-start | bytes 3211264 | tf_op jit(solution)/shard_map/all_to_all | solution.py:130
  171.3 1.1 fusion.26
  172.3 1.1 fusion.25
  174.5 1.1 fusion.23
  176.6 1.1 fusion.21
  178.7 1.1 fusion.19
  182.0 1.1 fusion.16
  186.1 1.1 fusion.12
  187.2 1.1 fusion.11
  188.2 1.1 fusion.10
  189.3 15.8 %all-to-all-done.2 = bf16[8,2,14,14,256]{4,1,3,2,0:T(2,128)(2,1)S(1)} async-done(((bf16[8,2,14,14,256]{4,1,3,2,0:T(2,128)(2,1)}), bf16[8,2,14,14,256]{4,1,3,2,0:T(2,128)(2,1)S(1)}, u32[]{:S(2)}, u32[]{:S(2)}) %all-to-all-start.2) | async-done | bytes 1605664 | tf_op jit(solution)/shard_map/all_to_all | solution.py:130
  205.4 1.2 reshape.131
  207.3 1.5 reshape.132
  208.9 90.9 %while.14 = (s32[]{:T(128)}, f32[16,32,256]{2,0,1:T(8,128)S(1)}, s32[16]{0:T(128)S(1)}, s32[16]{0:T(128)S(1)}, bf16[16,14,14,256]{3,2,1,0:T(8,128)(2,1)S(1)}, /*index=5*/s32[]{:T(128)}, s32[]{:T(128)}, s32[]{:T(128)}, s32[]{:T(128)}) while((s32[]{:T(128)}, f32[16,32,256]{2,0,1:T(8,128)S(1)}, s32[16]{0:T(128)S(1)}, s32[16]{0:T(128)S(1)}, ...), condition=%wide.region_2.3_spmd, body=%wide.region_1.2_spmd.sunk | while | flops 100360 | bytes 1706193 | solution.py:147
  300.1 1.9 collective-permute-start.4
  302.0 5.8 %collective-permute-start.5 = (bf16[1,32,256]{2,0,1:T(2,128)(2,1)S(1)}, bf16[1,32,256]{2,0,1:T(2,128)(2,1)S(1)}, u32[]{:S(2)}, u32[]{:S(2)}) collective-permute-start(bf16[1,32,256]{2,0,1:T(2,128)(2,1)S(1)} %get-tuple-element.160), channel_id=1, source_target_pairs={{8,0},{16,8},{24,16},{32,24},{40,32},{48,40},{56,48},{64,56},{72,6... | collective-permute-start | bytes 49160 | tf_op jit(solution)/shard_map/ppermute | solution.py:18
  307.8 155.4 %all-reduce.5.cloned.1.call-done = (f32[3,3,256,256]{3,2,1,0:T(8,128)}, f32[3,3,256,256]{3,2,1,0:T(8,128)}) async-done(((f32[3,3,256,256]{3,2,1,0:T(8,128)}, f32[3,3,256,256]{3,2,1,0:T(8,128)}), (f32[3,3,256,256]{3,2,1,0:T(8,128)}, f32[3,3,256,256]{3,2,1,0:T(8,128)})) %all-reduce.5.cloned.1.call-update) | async-done | bytes 4718608 | tf_op jit(solution)/shard_map/psum | solution.py:135
  463.2 3.4 broadcast_multiply_fusion.1
  466.7 5.5 %collective-permute-start.6 = (bf16[18,1,256]{2,0,1:T(8,128)(2,1)S(1)}, bf16[18,1,256]{2,0,1:T(8,128)(2,1)S(1)}, u32[]{:S(2)}, u32[]{:S(2)}) collective-permute-start(bf16[18,1,256]{2,0,1:T(8,128)(2,1)S(1)} %get-tuple-element.155), channel_id=1, source_target_pairs={{0,1},{1,2},{2,3},{3,4},{4,5},{5,6},{6,7},{8,9},{9,10},{10,11},{11... | collective-permute-start | bytes 27656 | tf_op jit(solution)/shard_map/ppermute | solution.py:17
  472.1 1.9 collective-permute-start.7
  474.1 1.6 broadcast_multiply_fusion
  475.7 3.2 collective-permute-done.7
  (279 shorter events, 81.1 us)
Async XLA Ops:
  7.2 137.5 %copy-start = (bf16[3,3,256,256]{3,2,1,0:T(8,128)(2,1)S(1)}, bf16[3,3,256,256]{3,2,1,0:T(8,128)(2,1)}, u32[]{:S(2)}) copy-start(bf16[3,3,256,256]{3,2,1,0:T(8,128)(2,1)} %param.13) | copy-start | bytes 3538948
  8.0 12.5 %collective-permute-start.1 = (bf16[1,32,256]{2,1,0:T(8,128)(2,1)S(1)}, bf16[1,32,256]{2,1,0:T(8,128)(2,1)S(1)}, u32[]{:S(2)}, u32[]{:S(2)}) collective-permute-start(bf16[1,32,256]{2,1,0:T(8,128)(2,1)S(1)} %get-tuple-element.161), channel_id=1, source_target_pairs={{8,0},{16,8},{24,16},{32,24},{40,32},{48,40},{56,48},{64,56},{72,6... | collective-permute-start | bytes 49160 | tf_op jit(solution)/shard_map/ppermute | solution.py:18
  12.3 7.2 %collective-permute-start = (bf16[1,32,256]{2,1,0:T(8,128)(2,1)S(1)}, bf16[1,32,256]{2,1,0:T(8,128)(2,1)S(1)}, u32[]{:S(2)}, u32[]{:S(2)}) collective-permute-start(bf16[1,32,256]{2,1,0:T(8,128)(2,1)S(1)} %get-tuple-element.162), channel_id=1, source_target_pairs={{0,8},{8,16},{16,24},{24,32},{32,40},{40,48},{48,56},{56,64},{64,7... | collective-permute-start | bytes 49160 | tf_op jit(solution)/shard_map/ppermute | solution.py:17
  20.5 12.6 %copy-start.22 = (bf16[3,3,256,256]{3,2,1,0:T(8,128)(2,1)S(1)}, bf16[3,3,256,256]{3,2,1,0:T(8,128)(2,1)}, u32[]{:S(2)}) copy-start(bf16[3,3,256,256]{3,2,1,0:T(8,128)(2,1)} %param.11) | copy-start | bytes 3538948
  20.5 12.6 %copy-start.25 = (pred[8,5]{0,1:T(8,128)(4,1)S(1)}, pred[8,5]{0,1:T(8,128)(4,1)}, u32[]{:S(2)}) copy-start(pred[8,5]{0,1:T(8,128)(4,1)} %constant.124) | copy-start | bytes 124
  20.6 7.1 %collective-permute-start.2 = (bf16[18,1,256]{2,1,0:T(2,128)(2,1)S(1)}, bf16[18,1,256]{2,1,0:T(2,128)(2,1)S(1)}, u32[]{:S(2)}, u32[]{:S(2)}) collective-permute-start(bf16[18,1,256]{2,1,0:T(2,128)(2,1)S(1)} %get-tuple-element.157), channel_id=1, source_target_pairs={{0,1},{1,2},{2,3},{3,4},{4,5},{5,6},{6,7},{8,9},{9,10},{10,11},{11... | collective-permute-start | bytes 27656 | tf_op jit(solution)/shard_map/ppermute | solution.py:17
  25.7 6.9 %collective-permute-start.3 = (bf16[18,1,256]{2,1,0:T(2,128)(2,1)S(1)}, bf16[18,1,256]{2,1,0:T(2,128)(2,1)S(1)}, u32[]{:S(2)}, u32[]{:S(2)}) collective-permute-start(bf16[18,1,256]{2,1,0:T(2,128)(2,1)S(1)} %get-tuple-element.158), channel_id=1, source_target_pairs={{1,0},{2,1},{3,2},{4,3},{5,4},{6,5},{7,6},{9,8},{10,9},{11,10},{12... | collective-permute-start | bytes 27656 | tf_op jit(solution)/shard_map/ppermute | solution.py:18
  34.3 0.8 copy-start.2
  87.6 5.2 %copy-start.24 = (s32[16,1]{0,1:T(1,128)S(1)}, s32[16,1]{0,1:T(1,128)}, u32[]{:S(2)}) copy-start(s32[16,1]{0,1:T(1,128)} %param.16) | copy-start | bytes 196
  87.6 38.8 %all-to-all-start.1 = ((bf16[8,2,14,14,256]{4,1,3,2,0:T(2,128)(2,1)}), bf16[8,2,14,14,256]{4,1,3,2,0:T(2,128)(2,1)}, u32[]{:S(2)}, u32[]{:S(2)}) async-start(bf16[8,2,14,14,256]{4,1,3,2,0:T(2,128)(2,1)} %copy.100), calls=%async_computation.1 | async-start | bytes 3211264 | tf_op jit(solution)/shard_map/all_to_all | solution.py:109
  126.4 11.1 %all-to-all-start = ((bf16[8,2,4]{2,1,0:T(2,128)(2,1)}), bf16[8,2,4]{2,1,0:T(2,128)(2,1)S(1)}, u32[]{:S(2)}, u32[]{:S(2)}) async-start(bf16[8,2,4]{2,1,0:T(2,128)(2,1)} %bitcast.9), calls=%async_computation | async-start | bytes 8192 | tf_op jit(solution)/shard_map/all_to_all | solution.py:110
  140.6 12.0 %copy-start.8 = (bf16[4,14,14,256]{3,2,1,0:T(8,128)(2,1)}, bf16[4,14,14,256]{3,2,1,0:T(8,128)(2,1)S(1)}, u32[]{:S(2)}) copy-start(bf16[4,14,14,256]{3,2,1,0:T(8,128)(2,1)S(1)} %reshape.128) | copy-start | bytes 1204228
  140.6 0.7 copy-start.17
  141.0 1.3 copy-start.20
  143.5 1.2 copy-start.13
  148.5 0.8 copy-start.10
  149.3 1.2 copy-start.14
  152.6 1.1 copy-start.6
  152.6 1.1 copy-start.12
  153.7 2.4 copy-start.21
  164.4 6.9 %copy-start.7 = (bf16[14,4,16,256]{3,2,1,0:T(8,128)(2,1)S(1)}, bf16[14,4,16,256]{3,2,1,0:T(8,128)(2,1)}, u32[]{:S(2)}) copy-start(bf16[14,4,16,256]{3,2,1,0:T(8,128)(2,1)} %copy-done.6) | copy-start | bytes 1376260
  164.4 6.9 %copy-start.9 = (bf16[4,14,14,256]{3,2,1,0:T(8,128)(2,1)S(1)}, bf16[4,14,14,256]{3,2,1,0:T(8,128)(2,1)}, u32[]{:S(2)}) copy-start(bf16[4,14,14,256]{3,2,1,0:T(8,128)(2,1)} %copy-done.8) | copy-start | bytes 1204228
  164.4 40.7 %all-to-all-start.2 = ((bf16[8,2,14,14,256]{4,1,3,2,0:T(2,128)(2,1)}), bf16[8,2,14,14,256]{4,1,3,2,0:T(2,128)(2,1)S(1)}, u32[]{:S(2)}, u32[]{:S(2)}) async-start(bf16[8,2,14,14,256]{4,1,3,2,0:T(2,128)(2,1)} %copy.109), calls=%async_computation.2 | async-start | bytes 3211264 | tf_op jit(solution)/shard_map/all_to_all | solution.py:130
  171.3 291.9 %all-reduce.5.cloned.1.call-start = ((), (), s32[]{:S(2)}) async-start(), calls=%async_computation.3 | async-start | bytes 9437184 | tf_op jit(solution)/shard_map/psum | solution.py:135
  173.4 1.0 copy-start.15
  173.4 1.1 copy-start.16
  178.7 1.1 copy-start.5
  178.7 1.2 copy-start.11
  207.3 1.6 copy-start.18
  207.3 1.6 copy-start.19
  208.9 90.9 %copy-start.3 = (f32[16,8,5,256]{3,0,2,1:T(8,128)S(1)}, f32[16,8,5,256]{3,0,2,1:T(8,128)}, u32[]{:S(2)}) copy-start(f32[16,8,5,256]{3,0,2,1:T(8,128)} %copy-done.2) | copy-start | bytes 1966084
  300.1 166.5 %collective-permute-start.4 = (bf16[1,32,256]{2,0,1:T(2,128)(2,1)S(1)}, bf16[1,32,256]{2,0,1:T(2,128)(2,1)S(1)}, u32[]{:S(2)}, u32[]{:S(2)}) collective-permute-start(bf16[1,32,256]{2,0,1:T(2,128)(2,1)S(1)} %get-tuple-element.159), channel_id=1, source_target_pairs={{0,8},{8,16},{16,24},{24,32},{32,40},{40,48},{48,56},{56,64},{64,7... | collective-permute-start | bytes 49160 | tf_op jit(solution)/shard_map/ppermute | solution.py:17
  302.0 164.6 %collective-permute-start.5 = (bf16[1,32,256]{2,0,1:T(2,128)(2,1)S(1)}, bf16[1,32,256]{2,0,1:T(2,128)(2,1)S(1)}, u32[]{:S(2)}, u32[]{:S(2)}) collective-permute-start(bf16[1,32,256]{2,0,1:T(2,128)(2,1)S(1)} %get-tuple-element.160), channel_id=1, source_target_pairs={{8,0},{16,8},{24,16},{32,24},{40,32},{48,40},{56,48},{64,56},{72,6... | collective-permute-start | bytes 49160 | tf_op jit(solution)/shard_map/ppermute | solution.py:18
  463.2 10.9 %copy-start.4 = (f32[3,3,256,256]{3,2,1,0:T(8,128)S(1)}, f32[3,3,256,256]{3,2,1,0:T(8,128)}, u32[]{:S(2)}) copy-start(f32[3,3,256,256]{3,2,1,0:T(8,128)} %get-tuple-element.146) | copy-start | bytes 7077892
  466.7 9.0 %collective-permute-start.6 = (bf16[18,1,256]{2,0,1:T(8,128)(2,1)S(1)}, bf16[18,1,256]{2,0,1:T(8,128)(2,1)S(1)}, u32[]{:S(2)}, u32[]{:S(2)}) collective-permute-start(bf16[18,1,256]{2,0,1:T(8,128)(2,1)S(1)} %get-tuple-element.155), channel_id=1, source_target_pairs={{0,1},{1,2},{2,3},{3,4},{4,5},{5,6},{6,7},{8,9},{9,10},{10,11},{11... | collective-permute-start | bytes 27656 | tf_op jit(solution)/shard_map/ppermute | solution.py:17
  472.1 6.8 %collective-permute-start.7 = (bf16[18,1,256]{2,0,1:T(8,128)(2,1)S(1)}, bf16[18,1,256]{2,0,1:T(8,128)(2,1)S(1)}, u32[]{:S(2)}, u32[]{:S(2)}) collective-permute-start(bf16[18,1,256]{2,0,1:T(8,128)(2,1)S(1)} %get-tuple-element.156), channel_id=1, source_target_pairs={{1,0},{2,1},{3,2},{4,3},{5,4},{6,5},{7,6},{9,8},{10,9},{11,10},{12... | collective-permute-start | bytes 27656 | tf_op jit(solution)/shard_map/ppermute | solution.py:18
  475.7 3.7 copy-start.23
  479.4 1.9 copy-start.1
Sparse Core Ops, SparseCore 0:
  189.4 273.7 all-reduce.4
where the time goes:
time: 491 us; the launch traced here: 488 us
  waiting for transfers between devices  214 us (44%)
  local copies, waits for them, and re-layouts  104 us (21%)
  loops' own time  63.1 us (13%)
  starting transfers between devices  47.2 us (10%)
  matrix products  30.9 us (6%)
  between operations  14.8 us (3%)
  other arithmetic  13.8 us (3%)
    psum x1, waiting for transfers between devices, body(): lax.psum((first_local, second_local), ('row', 'col'))  155 us
    another operation x1, loops' own time, body(): lax.fori_loop(0, slot_count, add_box, jnp.zeros((tile_rows, tile_cols, ch...  62.9 us
    gather x64, local copies, waits for them, and re-layouts  41.8 us
    all_to_all x1, waiting for transfers between devices, body(): lax.all_to_all(outgoing, 'col', split_axis=0, concat_axis=0, tiled=True)  32.7 us
    dot_general x18, matrix products, weight_grad(): lax.dot_general(window, flat_delta, (((0,), (0,)), ((), ())), preferred_e...  18.9 us
    all_to_all x1, waiting for transfers between devices, body(): lax.all_to_all(sent_back, 'col', split_axis=0, concat_axis=0, tiled=True)  15.8 us
    ppermute x4, starting transfers between devices, padded_2(): before = lax.ppermute(last, axis, up)  14.5 us
    ppermute x4, starting transfers between devices, padded_2(): after = lax.ppermute(leading, axis, down)  13.9 us
  transfers between devices with their start and end apart: 12, of which 7 were waited for; matrix products, arithmetic and copies ran while one was open for 13% of the time, Pallas kernels for 0%

commit v1 on v0

--- a/solution.py
+++ b/solution.py
@@ -132,7 +132,13 @@
         slot_count, box_side, box_side, channels
     )
     first_local = weight_grad(box_input, delta_one)
-    first_sum, second_sum = lax.psum((first_local, second_local), ("row", "col"))
+
+    def blocks_refer(packet, peer_axis, which_axis):
+        for w in (peer_axis, which_axis):
+            packet = lax.psum(packet, axis_name=w)
+        return packet
+
+    first_sum, second_sum = blocks_refer((first_local, second_local), "col", "row")
 
     def add_box(slot, running):
         current = lax.dynamic_slice(

time: 491 us -> 474 us (0.965)
  waiting for transfers between devices: 214 us -> 172 us
  other arithmetic: 13.8 us -> 27.3 us
  local copies, waits for them, and re-layouts: 104 us -> 117 us
    psum x1 -> x2, waiting for transfers between devices: 155 us -> 72.9 us  [blocks_refer(): packet = lax.psum(packet, axis_name=w)]
    all_to_all x1, waiting for transfers between devices: 15.8 us -> 54.2 us  [body(): lax.all_to_all(sent_back, 'col', split_axis=0, concat_axis=0, tiled=True)]
    add x16, other arithmetic: 2.09 us -> 16.5 us  [add_box(): current + slot_grads[slot].astype(jnp.float32)]
    unnamed x56 -> x64, local copies, waits for them, and re-layouts: 5.42 us -> 10.3 us
  transfers between devices with their start and end apart: 12 -> 13, of which waited for: 7 -> 8; matrix products, arithmetic and copies ran while one was open for 13% -> 16% of each run, Pallas kernels for 0% -> 0%
where the time goes in v1:
time: 474 us; the launch traced here: 470 us
  waiting for transfers between devices  172 us (36%)
  local copies, waits for them, and re-layouts  117 us (25%)
  loops' own time  63.1 us (13%)
  starting transfers between devices  46.3 us (10%)
  matrix products  29.9 us (6%)
  other arithmetic  27.3 us (6%)
  between operations  14.8 us (3%)
    psum x2, waiting for transfers between devices, blocks_refer(): packet = lax.psum(packet, axis_name=w)  72.9 us
    another operation x1, loops' own time, body(): lax.fori_loop(0, slot_count, add_box, jnp.zeros((tile_rows, tile_cols, ch...  62.9 us
    all_to_all x1, waiting for transfers between devices, body(): lax.all_to_all(sent_back, 'col', split_axis=0, concat_axis=0, tiled=True)  54.2 us
    gather x64, local copies, waits for them, and re-layouts  42.1 us
    all_to_all x1, waiting for transfers between devices, body(): lax.all_to_all(outgoing, 'col', split_axis=0, concat_axis=0, tiled=True)  32.5 us
    add x16, other arithmetic, add_box(): current + slot_grads[slot].astype(jnp.float32)  16.5 us
    ppermute x4, starting transfers between devices, padded_2(): after = lax.ppermute(leading, axis, down)  15.3 us
    dot_general x18, matrix products, weight_grad(): lax.dot_general(window, flat_delta, (((0,), (0,)), ((), ())), preferred_e...  15.2 us
  transfers between devices with their start and end apart: 13, of which 8 were waited for; matrix products, arithmetic and copies ran while one was open for 16% of the time, Pallas kernels for 0%

profile of v1, /device:TPU:98, one launch (start us, length us, event | category | flops | bytes accessed | tf_op | source)
XLA Modules:
  0.0 470.2 jit_solution(2804797186573654058)
XLA Ops:
  8.0 4.3 collective-permute-start.1
  12.3 1.9 collective-permute-start
  17.8 1.7 collective-permute-done
  20.6 5.2 %collective-permute-start.2 = (bf16[18,1,256]{2,1,0:T(2,128)(2,1)S(1)}, bf16[18,1,256]{2,1,0:T(2,128)(2,1)S(1)}, u32[]{:S(2)}, u32[]{:S(2)}) collective-permute-start(bf16[18,1,256]{2,1,0:T(2,128)(2,1)S(1)} %get-tuple-element.159), channel_id=1, source_target_pairs={{0,1},{1,2},{2,3},{3,4},{4,5},{5,6},{6,7},{8,9},{9,10},{10,11},{11... | collective-permute-start | bytes 27656 | tf_op jit(solution)/shard_map/ppermute | solution.py:17
  25.7 1.9 collective-permute-start.3
  27.7 4.9 %collective-permute-done.3 = bf16[18,1,256]{2,1,0:T(2,128)(2,1)S(1)} collective-permute-done((bf16[18,1,256]{2,1,0:T(2,128)(2,1)S(1)}, bf16[18,1,256]{2,1,0:T(2,128)(2,1)S(1)}, u32[]{:S(2)}, u32[]{:S(2)}) %collective-permute-start.3) | collective-permute-done | bytes 9248 | tf_op jit(solution)/shard_map/ppermute | solution.py:18
  35.2 42.3 %while.15 = (s32[]{:T(128)}, bf16[16,32,256]{2,0,1:T(8,128)(2,1)S(1)}, s32[16,3]{0,1:T(4,128)S(1)}, bf16[16,14,14,256]{3,2,1,0:T(8,128)(2,1)}, s32[]{:T(128)}) while((s32[]{:T(128)}, bf16[16,32,256]{2,0,1:T(8,128)(2,1)S(1)}, s32[16,3]{0,1:T(4,128)S(1)}, bf16[16,14,14,256]{3,2,1,0:T(8,128)(2,1)}, s32[]{:T(128)}) %tuple.61), condition=%wide.while_cond, body=%wide.while_body.sunk | while | flops 2 | bytes 415869 | solution.py:105
  35.9 1.3 constant_dynamic-slice_fusion.8
  38.6 1.3 constant_dynamic-slice_fusion.8
  41.2 1.3 constant_dynamic-slice_fusion.8
  43.8 1.3 constant_dynamic-slice_fusion.8
  46.5 1.3 constant_dynamic-slice_fusion.8
  49.1 1.3 constant_dynamic-slice_fusion.8
  51.8 1.3 constant_dynamic-slice_fusion.8
  54.4 1.3 constant_dynamic-slice_fusion.8
  57.1 1.3 constant_dynamic-slice_fusion.8
  59.7 1.3 constant_dynamic-slice_fusion.8
  62.3 1.3 constant_dynamic-slice_fusion.8
  65.0 1.3 constant_dynamic-slice_fusion.8
  67.6 1.3 constant_dynamic-slice_fusion.8
  70.3 1.3 constant_dynamic-slice_fusion.8
  72.9 1.3 constant_dynamic-slice_fusion.8
  75.5 1.3 constant_dynamic-slice_fusion.8
  77.5 2.4 reshape.125
  79.9 1.7 convolution_convert_fusion.1
  81.7 2.6 reshape.126
  84.3 3.6 copy.100
  87.9 5.2 %all-to-all-start.1 = ((bf16[8,2,14,14,256]{4,1,3,2,0:T(2,128)(2,1)}), bf16[8,2,14,14,256]{4,1,3,2,0:T(2,128)(2,1)S(1)}, u32[]{:S(2)}, u32[]{:S(2)}) async-start(bf16[8,2,14,14,256]{4,1,3,2,0:T(2,128)(2,1)} %copy.100), calls=%async_computation.1 | async-start | bytes 3211264 | tf_op jit(solution)/shard_map/all_to_all | solution.py:109
  94.1 32.5 %all-to-all-done.1 = bf16[8,2,14,14,256]{4,1,3,2,0:T(2,128)(2,1)S(1)} async-done(((bf16[8,2,14,14,256]{4,1,3,2,0:T(2,128)(2,1)}), bf16[8,2,14,14,256]{4,1,3,2,0:T(2,128)(2,1)S(1)}, u32[]{:S(2)}, u32[]{:S(2)}) %all-to-all-start.1) | async-done | bytes 1605664 | tf_op jit(solution)/shard_map/all_to_all | solution.py:109
  126.7 6.7 %all-to-all-start = ((bf16[8,2,4]{2,1,0:T(2,128)(2,1)}), bf16[8,2,4]{2,1,0:T(2,128)(2,1)S(1)}, u32[]{:S(2)}, u32[]{:S(2)}) async-start(bf16[8,2,4]{2,1,0:T(2,128)(2,1)} %bitcast.9), calls=%async_computation | async-start | bytes 8192 | tf_op jit(solution)/shard_map/all_to_all | solution.py:110
  133.4 1.7 copy.101
  135.1 2.1 reshape.127
  137.7 1.8 convolution_convert_fusion.3
  142.5 1.2 convolution_select_fusion.1
  143.8 1.1 select_bitcast_fusion.1
  145.0 1.3 add_multiply_fusion
  149.7 1.3 fusion.8
  153.3 1.4 fusion.27
  154.8 1.2 copy.117
  156.0 1.2 reshape.173
  158.0 1.9 reshape.134
  159.9 1.4 fusion.26
  165.4 1.3 fusion.18
  170.1 1.2 fusion.14
  177.8 1.3 convolution_convert_fusion.4
  180.1 1.7 convolution_convert_fusion.2
  181.8 2.6 reshape.130
  184.5 3.7 copy.109
  188.2 7.4 %all-to-all-start.2 = ((bf16[8,2,14,14,256]{4,1,3,2,0:T(2,128)(2,1)}), bf16[8,2,14,14,256]{4,1,3,2,0:T(2,128)(2,1)}, u32[]{:S(2)}, u32[]{:S(2)}) async-start(bf16[8,2,14,14,256]{4,1,3,2,0:T(2,128)(2,1)} %copy.109), calls=%async_computation.2 | async-start | bytes 3211264 | tf_op jit(solution)/shard_map/all_to_all | solution.py:130
  195.6 54.2 %all-to-all-done.2 = bf16[8,2,14,14,256]{4,1,3,2,0:T(2,128)(2,1)} async-done(((bf16[8,2,14,14,256]{4,1,3,2,0:T(2,128)(2,1)}), bf16[8,2,14,14,256]{4,1,3,2,0:T(2,128)(2,1)}, u32[]{:S(2)}, u32[]{:S(2)}) %all-to-all-start.2) | async-done | bytes 1605664 | tf_op jit(solution)/shard_map/all_to_all | solution.py:130
  249.8 1.7 copy.110
  251.5 2.1 reshape.131
  253.6 2.1 convolution_convert_fusion
  255.7 2.4 reshape.132
  258.1 72.9 %all-reduce.9.cloned.1.call-done = (f32[3,3,256,256]{3,2,1,0:T(8,128)}, f32[3,3,256,256]{3,2,1,0:T(8,128)}) async-done(((f32[3,3,256,256]{3,2,1,0:T(8,128)}, f32[3,3,256,256]{3,2,1,0:T(8,128)}), (f32[3,3,256,256]{3,2,1,0:T(8,128)}, f32[3,3,256,256]{3,2,1,0:T(8,128)})) %all-reduce.9.cloned.1.call-update) | async-done | bytes 4718608 | tf_op jit(solution)/shard_map/psum | solution.py:138
  331.7 105.3 %while.14 = (s32[]{:T(128)}, f32[16,32,256]{2,0,1:T(8,128)S(1)}, s32[16]{0:T(128)S(1)}, s32[16]{0:T(128)S(1)}, bf16[16,14,14,256]{3,2,1,0:T(8,128)(2,1)}, /*index=5*/s32[]{:T(128)}, s32[]{:T(128)}, s32[]{:T(128)}, s32[]{:T(128)}) while((s32[]{:T(128)}, f32[16,32,256]{2,0,1:T(8,128)S(1)}, s32[16]{0:T(128)S(1)}, s32[16]{0:T(128)S(1)}, ...), condition=%wide.region_2.3_spmd, body=%wide.region_1.2_spmd.sunk | while | flops 100360 | bytes 1706193 | solution.py:153
  437.3 2.1 collective-permute-start.4
  439.4 5.8 %collective-permute-start.5 = (bf16[1,32,256]{2,0,1:T(2,128)(2,1)S(1)}, bf16[1,32,256]{2,0,1:T(2,128)(2,1)S(1)}, u32[]{:S(2)}, u32[]{:S(2)}) collective-permute-start(bf16[1,32,256]{2,0,1:T(2,128)(2,1)S(1)} %get-tuple-element.162), channel_id=1, source_target_pairs={{8,0},{16,8},{24,16},{32,24},{40,32},{48,40},{56,48},{64,56},{72,6... | collective-permute-start | bytes 49160 | tf_op jit(solution)/shard_map/ppermute | solution.py:18
  445.1 1.6 collective-permute-done.5
  446.7 2.5 collective-permute-start.6
  449.2 3.3 collective-permute-start.7
  452.6 3.4 collective-permute-done.7
  458.3 3.4 broadcast_multiply_fusion.1
  461.8 1.6 broadcast_multiply_fusion
  (290 shorter events, 100.4 us)
Async XLA Ops:
  7.2 137.8 %copy-start = (bf16[3,3,256,256]{3,2,1,0:T(8,128)(2,1)S(1)}, bf16[3,3,256,256]{3,2,1,0:T(8,128)(2,1)}, u32[]{:S(2)}) copy-start(bf16[3,3,256,256]{3,2,1,0:T(8,128)(2,1)} %param.13) | copy-start | bytes 3538948
  8.0 12.5 %collective-permute-start.1 = (bf16[1,32,256]{2,1,0:T(8,128)(2,1)S(1)}, bf16[1,32,256]{2,1,0:T(8,128)(2,1)S(1)}, u32[]{:S(2)}, u32[]{:S(2)}) collective-permute-start(bf16[1,32,256]{2,1,0:T(8,128)(2,1)S(1)} %get-tuple-element.163), channel_id=1, source_target_pairs={{8,0},{16,8},{24,16},{32,24},{40,32},{48,40},{56,48},{64,56},{72,6... | collective-permute-start | bytes 49160 | tf_op jit(solution)/shard_map/ppermute | solution.py:18
  12.3 7.2 %collective-permute-start = (bf16[1,32,256]{2,1,0:T(8,128)(2,1)S(1)}, bf16[1,32,256]{2,1,0:T(8,128)(2,1)S(1)}, u32[]{:S(2)}, u32[]{:S(2)}) collective-permute-start(bf16[1,32,256]{2,1,0:T(8,128)(2,1)S(1)} %get-tuple-element.164), channel_id=1, source_target_pairs={{0,8},{8,16},{16,24},{24,32},{32,40},{40,48},{48,56},{56,64},{64,7... | collective-permute-start | bytes 49160 | tf_op jit(solution)/shard_map/ppermute | solution.py:17
  20.5 12.6 %copy-start.25 = (bf16[3,3,256,256]{3,2,1,0:T(8,128)(2,1)S(1)}, bf16[3,3,256,256]{3,2,1,0:T(8,128)(2,1)}, u32[]{:S(2)}) copy-start(bf16[3,3,256,256]{3,2,1,0:T(8,128)(2,1)} %param.11) | copy-start | bytes 3538948
  20.5 12.6 %copy-start.28 = (pred[8,5]{0,1:T(8,128)(4,1)S(1)}, pred[8,5]{0,1:T(8,128)(4,1)}, u32[]{:S(2)}) copy-start(pred[8,5]{0,1:T(8,128)(4,1)} %constant.124) | copy-start | bytes 124
  20.6 7.1 %collective-permute-start.2 = (bf16[18,1,256]{2,1,0:T(2,128)(2,1)S(1)}, bf16[18,1,256]{2,1,0:T(2,128)(2,1)S(1)}, u32[]{:S(2)}, u32[]{:S(2)}) collective-permute-start(bf16[18,1,256]{2,1,0:T(2,128)(2,1)S(1)} %get-tuple-element.159), channel_id=1, source_target_pairs={{0,1},{1,2},{2,3},{3,4},{4,5},{5,6},{6,7},{8,9},{9,10},{10,11},{11... | collective-permute-start | bytes 27656 | tf_op jit(solution)/shard_map/ppermute | solution.py:17
  25.7 6.9 %collective-permute-start.3 = (bf16[18,1,256]{2,1,0:T(2,128)(2,1)S(1)}, bf16[18,1,256]{2,1,0:T(2,128)(2,1)S(1)}, u32[]{:S(2)}, u32[]{:S(2)}) collective-permute-start(bf16[18,1,256]{2,1,0:T(2,128)(2,1)S(1)} %get-tuple-element.160), channel_id=1, source_target_pairs={{1,0},{2,1},{3,2},{4,3},{5,4},{6,5},{7,6},{9,8},{10,9},{11,10},{12... | collective-permute-start | bytes 27656 | tf_op jit(solution)/shard_map/ppermute | solution.py:18
  34.3 0.8 copy-start.3
  87.9 5.2 %copy-start.27 = (s32[16,1]{0,1:T(1,128)S(1)}, s32[16,1]{0,1:T(1,128)}, u32[]{:S(2)}) copy-start(s32[16,1]{0,1:T(1,128)} %param.16) | copy-start | bytes 196
  87.9 38.7 %all-to-all-start.1 = ((bf16[8,2,14,14,256]{4,1,3,2,0:T(2,128)(2,1)}), bf16[8,2,14,14,256]{4,1,3,2,0:T(2,128)(2,1)S(1)}, u32[]{:S(2)}, u32[]{:S(2)}) async-start(bf16[8,2,14,14,256]{4,1,3,2,0:T(2,128)(2,1)} %copy.100), calls=%async_computation.1 | async-start | bytes 3211264 | tf_op jit(solution)/shard_map/all_to_all | solution.py:109
  126.7 6.7 %copy-start.2 = (bf16[8,2,14,14,256]{4,1,3,2,0:T(2,128)(2,1)}, bf16[8,2,14,14,256]{4,1,3,2,0:T(2,128)(2,1)S(1)}, u32[]{:S(2)}) copy-start(bf16[8,2,14,14,256]{4,1,3,2,0:T(2,128)(2,1)S(1)} %all-to-all-done.1) | copy-start | bytes 4816900
  126.7 11.1 %all-to-all-start = ((bf16[8,2,4]{2,1,0:T(2,128)(2,1)}), bf16[8,2,4]{2,1,0:T(2,128)(2,1)S(1)}, u32[]{:S(2)}, u32[]{:S(2)}) async-start(bf16[8,2,4]{2,1,0:T(2,128)(2,1)} %bitcast.9), calls=%async_computation | async-start | bytes 8192 | tf_op jit(solution)/shard_map/all_to_all | solution.py:110
  133.4 197.7 %all-reduce.9.cloned.1.call-start = ((), (), s32[]{:S(2)}) async-start(), calls=%async_computation.4 | async-start | bytes 9437184 | tf_op jit(solution)/shard_map/psum | solution.py:138
  140.9 0.8 copy-start.9
  140.9 0.8 copy-start.20
  141.2 1.3 copy-start.23
  143.7 1.2 copy-start.14
  146.3 1.4 copy-start.17
  147.8 0.8 copy-start.11
  148.6 1.2 copy-start.15
  151.1 0.8 copy-start.7
  153.3 1.4 copy-start.13
  159.9 1.4 copy-start.10
  161.7 1.0 copy-start.18
  161.7 1.1 copy-start.19
  164.3 1.0 copy-start.12
  164.3 1.1 copy-start.16
  165.4 1.5 copy-start.6
  175.5 1.0 copy-start.8
  176.5 1.3 copy-start.24
  188.2 61.6 %all-to-all-start.2 = ((bf16[8,2,14,14,256]{4,1,3,2,0:T(2,128)(2,1)}), bf16[8,2,14,14,256]{4,1,3,2,0:T(2,128)(2,1)}, u32[]{:S(2)}, u32[]{:S(2)}) async-start(bf16[8,2,14,14,256]{4,1,3,2,0:T(2,128)(2,1)} %copy.109), calls=%async_computation.2 | async-start | bytes 3211264 | tf_op jit(solution)/shard_map/all_to_all | solution.py:130
  195.6 262.7 %all-reduce.7.cloned.1.call-start = ((), (), s32[]{:S(2)}) async-start(), calls=%async_computation.3 | async-start | bytes 9437184 | tf_op jit(solution)/shard_map/psum | solution.py:138
  331.0 0.7 copy-start.21
  331.0 0.7 copy-start.22
  331.7 105.3 %copy-start.4 = (f32[16,8,5,256]{3,0,2,1:T(8,128)S(1)}, f32[16,8,5,256]{3,0,2,1:T(8,128)}, u32[]{:S(2)}) copy-start(f32[16,8,5,256]{3,0,2,1:T(8,128)} %copy-done.3) | copy-start | bytes 1966084
  437.2 19.2 %copy-start.26 = (bf16[3,3,256,256]{3,2,1,0:T(8,128)(2,1)S(1)}, bf16[3,3,256,256]{3,2,1,0:T(8,128)(2,1)}, u32[]{:S(2)}) copy-start(bf16[3,3,256,256]{3,2,1,0:T(8,128)(2,1)} %param.11) | copy-start | bytes 3538948
  437.2 19.2 %copy-start.29 = (pred[8,5]{0,1:T(8,128)(4,1)S(1)}, pred[8,5]{0,1:T(8,128)(4,1)}, u32[]{:S(2)}) copy-start(pred[8,5]{0,1:T(8,128)(4,1)} %constant.124) | copy-start | bytes 124
  437.3 7.8 %collective-permute-start.4 = (bf16[1,32,256]{2,0,1:T(2,128)(2,1)S(1)}, bf16[1,32,256]{2,0,1:T(2,128)(2,1)S(1)}, u32[]{:S(2)}, u32[]{:S(2)}) collective-permute-start(bf16[1,32,256]{2,0,1:T(2,128)(2,1)S(1)} %get-tuple-element.161), channel_id=1, source_target_pairs={{0,8},{8,16},{16,24},{24,32},{32,40},{40,48},{48,56},{56,64},{64,7... | collective-permute-start | bytes 49160 | tf_op jit(solution)/shard_map/ppermute | solution.py:17
  439.4 7.3 %collective-permute-start.5 = (bf16[1,32,256]{2,0,1:T(2,128)(2,1)S(1)}, bf16[1,32,256]{2,0,1:T(2,128)(2,1)S(1)}, u32[]{:S(2)}, u32[]{:S(2)}) collective-permute-start(bf16[1,32,256]{2,0,1:T(2,128)(2,1)S(1)} %get-tuple-element.162), channel_id=1, source_target_pairs={{8,0},{16,8},{24,16},{32,24},{40,32},{48,40},{56,48},{64,56},{72,6... | collective-permute-start | bytes 49160 | tf_op jit(solution)/shard_map/ppermute | solution.py:18
  446.7 5.9 %collective-permute-start.6 = (bf16[18,1,256]{2,0,1:T(8,128)(2,1)S(1)}, bf16[18,1,256]{2,0,1:T(8,128)(2,1)S(1)}, u32[]{:S(2)}, u32[]{:S(2)}) collective-permute-start(bf16[18,1,256]{2,0,1:T(8,128)(2,1)S(1)} %get-tuple-element.157), channel_id=1, source_target_pairs={{0,1},{1,2},{2,3},{3,4},{4,5},{5,6},{6,7},{8,9},{9,10},{10,11},{11... | collective-permute-start | bytes 27656 | tf_op jit(solution)/shard_map/ppermute | solution.py:17
  449.2 6.8 %collective-permute-start.7 = (bf16[18,1,256]{2,0,1:T(8,128)(2,1)S(1)}, bf16[18,1,256]{2,0,1:T(8,128)(2,1)S(1)}, u32[]{:S(2)}, u32[]{:S(2)}) collective-permute-start(bf16[18,1,256]{2,0,1:T(8,128)(2,1)S(1)} %get-tuple-element.158), channel_id=1, source_target_pairs={{1,0},{2,1},{3,2},{4,3},{5,4},{6,5},{7,6},{9,8},{10,9},{11,10},{12... | collective-permute-start | bytes 27656 | tf_op jit(solution)/shard_map/ppermute | solution.py:18
  458.3 3.4 copy-start.5
  461.8 1.6 copy-start.1
Sparse Core Ops, SparseCore 0:
  175.7 155.3 all-reduce.8
  334.5 121.5 all-reduce.6
